TPU v7x, 128 devices: a whole 4x4x4 slice. The times are simulated.
128 devices in a mesh: gx: 16 (over z, y_hi, core), gy: 8 (over x, y_lo).
Axes of the slice: x: 4, y: 4 (y_hi: 2, y_lo: 2; y = y_hi * 2 + y_lo), z: 4, core: 2. Of those that a mesh axis runs over, the one named last changes fastest.
Arguments:
- blocks: bfloat16 [2, 16384, 2048], P(None, ('gx', 'gy')), may hold values from 0.19921875 to 4
- owner_route: int32 [2, 16384, 1], P(None, ('gx', 'gy')), may hold values from 0 to 127; in each aligned block of 128 rows (0 to 127, 128 to 255, ..., all dimensions but the last counted through in order) at most 2 rows name the same one
- block_slot: int32 [2, 16384], P(None, ('gx', 'gy')), may hold values from 0 to 63
- estimate: float32 [2, 4096, 2048], P(None, 'gx', 'gy'), may hold values from 0.5 to 2
- background: float32 [2, 2], replicated, may hold values from 0.2 to 2
- psf_taps: float32 [2, 4, 2, 17], replicated, may hold values from 0.05 to 1
- psf_index: int32 [2, 2], replicated, may hold values from 0 to 3
Outputs:
- deconvolved: float32 [2, 4096, 2048], P(None, 'gx', 'gy')
Inputs may be any that keep to these rules, and one draw needn't show every extreme that they name: `owner_route`: among the 128 blocks of one view held by one device (aligned runs of rows along dimension 1), no tile is named more than 2 times.
All inputs are finite; a program needn't handle non-finite values.
Results may differ from a plain program's by a relative error of at most 0.0008.
Values may be sent and summed in bfloat16 or wider, within the bound.
A program may use at most 64 MiB of HBM per device.

v0:
```python
import jax
import jax.numpy as jnp
from jax import lax
from jax.experimental import pallas as pl
from jax.experimental.pallas import tpu as pltpu
from jax.sharding import PartitionSpec as P

MESH = pl.DeviceIdType.MESH
F32 = jnp.float32
BF16 = jnp.bfloat16

N_GX, N_GY = 16, 8
DEVICES = N_GX * N_GY
TILE = 256
TAPS = 17
STEP, STEP_INVERSE = 27, 19
GROUP = 16
GROUPS = DEVICES // GROUP
CHUNK = 8
HALO_PARTS = (
    (0, 32, 1, 0),
    (32, 32, -1, 0),
    (64, 64, 0, 1),
    (128, 64, 0, -1),
    (192, 16, 1, 1),
    (208, 16, 1, -1),
    (224, 16, -1, 1),
    (240, 16, -1, -1),
)
HALO_ROWS = 256


def iota(shape, dim):
    return lax.broadcasted_iota(jnp.int32, shape, dim)


def dot(a, b):
    return jnp.dot(a, b, preferred_element_type=F32)


def split(a):
    high = a.astype(BF16)
    return high, (a - high.astype(F32)).astype(BF16)


def torus_position():
    gx, gy = lax.axis_index("gx"), lax.axis_index("gy")
    return gy // 2, ((gx // 2) % 2) * 2 + gy % 2, gx // 4, gx % 2


def partner(slot, here):
    x, y, z, core = here
    shift = (slot * STEP) % DEVICES
    core = (core + shift % 2) % 2
    x = (x + (shift // 2) % 4) % 4
    y = (y + (shift // 8) % 4) % 4
    z = (z + shift // 32) % 4
    return z * 4 + (y // 2) * 2 + core, x * 2 + y % 2


def slot_of(tile, here):
    x, y, z, core = here
    gx, gy = tile >> 3, tile & 7
    d_core = ((gx & 1) - core) & 1
    dx = ((gy >> 1) - x) & 3
    dy = ((((gx >> 1) & 1) * 2 + (gy & 1)) - y) & 3
    dz = ((gx >> 2) - z) & 3
    return ((d_core + 2 * dx + 8 * dy + 32 * dz) * STEP_INVERSE) & (DEVICES - 1)


def kernel(
    blocks,
    owners,
    places,
    estimate,
    background,
    psf_taps,
    psf_index,
    result,
    staged,
    outgoing,
    incoming,
    ids_out,
    ids_in,
    landing,
    summed,
    measured,
    inverse,
    ratio,
    shuffle,
    halo_out,
    halo_in,
    fwd_y,
    fwd_y_halo,
    fwd_x,
    fwd_x_halo,
    back_y,
    back_y_halo,
    back_x,
    back_x_halo,
    ready,
    data_sent,
    data_here,
    ids_sent,
    ids_here,
    halo_sent,
    halo_here,
):
    gx, gy = lax.axis_index("gx"), lax.axis_index("gy")
    here = torus_position()
    barrier = pltpu.get_barrier_semaphore()

    for step in range(1, N_GX):
        pl.semaphore_signal(
            barrier, inc=1, device_id=((gx + step) % N_GX, gy), device_id_type=MESH
        )
    for step in range(1, N_GY):
        pl.semaphore_signal(
            barrier, inc=1, device_id=(gx, (gy + step) % N_GY), device_id_type=MESH
        )

    def halo_copy(part, exchange, plane):
        start, rows, to_x, to_y = part
        return pltpu.make_async_remote_copy(
            src_ref=halo_out.at[exchange, plane, pl.ds(start, rows)],
            dst_ref=halo_in.at[exchange, plane, pl.ds(start, rows)],
            send_sem=halo_sent.at[exchange, plane],
            recv_sem=halo_here.at[exchange, plane],
            device_id=((gx + to_x + N_GX) % N_GX, (gy + to_y + N_GY) % N_GY),
            device_id_type=MESH,
        )

    def send_halo(exchange, plane):
        for part in HALO_PARTS:
            halo_copy(part, exchange, plane).start()

    def pack_halo(fields, by_rows, exchange, plane):
        count = len(fields)
        out = halo_out.at[exchange, plane]

        def edge(ref, high, tile):
            if by_rows:
                return ref[pl.ds(248 if high else 0, 8), pl.ds(tile * 128, 128)]
            return ref[tile, pl.ds(31 if high else 0, 8, stride=32), :]

        def stack(parts):
            if count == 1:
                parts = parts + [jnp.zeros_like(parts[0])]
            return jnp.concatenate(parts, axis=0).astype(BF16)

        edges = {}
        for high in (True, False):
            for tile in range(2):
                edges[high, tile] = [edge(ref, high, tile) for ref in fields]
        for at, high in ((0, True), (32, False)):
            for tile in range(2):
                out[pl.ds(at + 16 * tile, 16)] = stack(edges[high, tile])
        for at, high_x, high_y in (
            (192, True, True),
            (208, True, False),
            (224, False, True),
            (240, False, False),
        ):
            tile, shift = (1, 8) if high_y else (0, 16)
            out[pl.ds(at, 16)] = stack(
                [
                    pltpu.roll(e, shift + 8 * v, 1)
                    for v, e in enumerate(edges[high_x, tile])
                ]
            )
        lane = iota((64, 128), 1)
        for at, high_y in ((64, True), (128, False)):
            total = jnp.zeros((64, 128), F32)
            for v, ref in enumerate(fields):
                for slab in range(4):
                    rows = pl.ds(64 * slab, 64)
                    if by_rows:
                        piece = ref[rows, pl.ds(128 if high_y else 0, 128)]
                    else:
                        piece = ref[1 if high_y else 0, rows, :]
                    first = 32 * slab + 8 * v + (0 if high_y else 16)
                    moved = pltpu.roll(piece, (first + (8 if high_y else 0)) % 128, 1)
                    total = jnp.where((lane >= first) & (lane < first + 8), moved, total)
            out[pl.ds(at, 64)] = total.astype(BF16)

    def wait_halo(exchange, plane):
        whole = halo_in.at[exchange, plane]
        pltpu.make_async_copy(whole, whole, halo_here.at[exchange, plane]).wait()

    def read_halo(exchange, plane):
        got = halo_in.at[exchange, plane]
        rows = jnp.concatenate(
            [
                jnp.concatenate([got[pl.ds(0, 16)], got[pl.ds(16, 16)]], axis=1),
                jnp.concatenate([got[pl.ds(32, 16)], got[pl.ds(48, 16)]], axis=1),
            ],
            axis=0,
        )
        lane = iota((16, 128), 1)
        corners = [
            jnp.where(
                lane < 16,
                got[pl.ds(at, 16)].astype(F32),
                got[pl.ds(at + 16, 16)].astype(F32),
            )
            for at in (192, 224)
        ]
        lane = iota((64, 128), 1)
        sides = jnp.where(
            lane % 32 < 16, got[pl.ds(64, 64)].astype(F32), got[pl.ds(128, 64)].astype(F32)
        )
        columns = jnp.concatenate(
            [sides] + [pltpu.roll(sides, 128 - 32 * slab, 1) for slab in range(1, 4)] + corners,
            axis=0,
        ).astype(BF16)
        return rows, columns[:, :32]

    slot_rows, rank_rows, rank_columns, place_columns = [], [], [], []
    sub, lane = iota((128, 128), 0), iota((128, 128), 1)
    for v in range(2):
        row = slot_of(owners[pl.ds(v, 1), :], here)
        across = jnp.broadcast_to(row, (128, 128))
        same = across == across.T
        slot_rows.append(row)
        rank_rows.append(
            jnp.sum(jnp.where(same & (sub < lane), 1.0, 0.0), axis=0, keepdims=True).astype(
                jnp.int32
            )
        )
        rank_columns.append(
            jnp.sum(jnp.where(same & (lane < sub), 1.0, 0.0), axis=1, keepdims=True)
        )
        place = places[pl.ds(v, 1), :]
        spot = ((place & 7) * 32 + (place >> 3) + 1).astype(F32)
        place_columns.append(jnp.broadcast_to(spot, (128, 128)).T)

    lane_view, lane_rank, lane_part = (lane >> 3) & 1, (lane >> 2) & 1, lane & 3
    ids = jnp.zeros((128, 128), F32)
    for v in range(2):
        taken = jnp.where(sub == slot_rows[v], 1.0, 0.0).astype(BF16)
        mine = (lane_view == v) & (lane_rank.astype(F32) == rank_columns[v])
        ids = ids + dot(taken, jnp.where(mine, place_columns[v], 0.0).astype(BF16))
    ids = jnp.where(ids > 0.0, ids + (lane_view * 256 + lane_part * 8 - 1).astype(F32), -1.0)
    ids_out[...] = ids.reshape(128, 1, 128)

    target = jnp.concatenate(
        [
            slot_rows[v] * 16 + v * 8 + rank_rows[v] * 4 + part
            for v in range(2)
            for part in range(4)
        ],
        axis=1,
    )
    for plane in range(2):
        for v in range(2):
            for part in range(4):
                staged[plane, pl.ds((v * 4 + part) * 128, 128), :] = blocks[
                    v, :, pl.ds(plane * 1024 + part * 256, 256)
                ]
    for plane in range(2):
        pack_halo([estimate.at[plane]], True, 0, plane)

    pl.semaphore_wait(barrier, N_GX + N_GY - 2)
    for step in range(1, N_GY):
        pl.semaphore_signal(
            ready, inc=1, device_id=(gx, (gy + step) % N_GY), device_id_type=MESH
        )
    pl.semaphore_wait(ready, N_GY - 1)

    for plane in range(2):
        send_halo(0, plane)

    def id_copy(slot):
        return pltpu.make_async_remote_copy(
            src_ref=ids_out.at[pl.ds(slot, 1)],
            dst_ref=ids_in.at[pl.ds(slot, 1)],
            send_sem=ids_sent,
            recv_sem=ids_here,
            device_id=partner(slot, here),
            device_id_type=MESH,
        )

    def data_copy(plane, slot):
        rows = pl.ds(pl.multiple_of(slot * 16, 16), 16)
        return pltpu.make_async_remote_copy(
            src_ref=outgoing.at[plane, rows],
            dst_ref=incoming.at[plane, rows],
            send_sem=data_sent.at[plane],
            recv_sem=data_here.at[plane, slot // GROUP],
            device_id=partner(slot, here),
            device_id_type=MESH,
        )

    @pl.loop(1, DEVICES)
    def _(slot):
        id_copy(slot).start()

    for plane in range(2):

        @pl.loop(0, DEVICES // CHUNK)
        def _(chunk):
            rows = CHUNK * 16
            wanted = iota((rows, 1024), 0) + chunk * rows
            pick = jnp.where(wanted == target, 1.0, 0.0).astype(BF16)
            outgoing[plane, pl.ds(pl.multiple_of(chunk * rows, rows), rows), :] = dot(
                pick, staged[plane]
            ).astype(BF16)
            for j in range(CHUNK):
                slot = chunk * CHUNK + j
                if j == 0:

                    @pl.when(chunk > 0)
                    def _():
                        data_copy(plane, slot).start()

                else:
                    data_copy(plane, slot).start()

    def bands(v, plane, axis, reverse):
        kernel_index = psf_index[v, plane]
        wide = iota((8, 512), 1)
        taps = jnp.zeros((8, 512), F32)
        total = jnp.zeros((8, 512), F32)
        for t in range(TAPS):
            value = psf_taps[v, kernel_index, axis, t]
            at = 120 + (TAPS - 1 - t if reverse else t)
            taps = jnp.where(wide == at, value, taps)
            total = total + value
        return taps / total

    def natural(first):
        rows = jnp.broadcast_to(first[0:1], (TILE, 512))
        return pltpu.roll(rows, 0, 1, stride=1, stride_axis=0)

    def reordered(first):
        rows = natural(first)
        for tile in range(4):
            shuffle[tile] = rows[:, tile * 128 : (tile + 1) * 128]
        return jnp.concatenate(
            [
                jnp.concatenate(
                    [
                        shuffle[tile, pl.ds(q * 8 + x8, 8, stride=32), :]
                        for tile in range(4)
                    ],
                    axis=1,
                )
                for x8 in range(8)
                for q in range(4)
            ],
            axis=0,
        )

    has_low_x = jnp.where(gx > 0, 1.0, 0.0)
    has_high_x = jnp.where(gx < N_GX - 1, 1.0, 0.0)
    has_low_y = jnp.where(gy > 0, 1.0, 0.0)
    has_high_y = jnp.where(gy < N_GY - 1, 1.0, 0.0)

    def put(ref, index, value):
        high, low = split(value)
        ref[(0,) + index] = high
        ref[(1,) + index] = low

    lane = iota((TILE, 128), 1)
    for plane in range(2):
        back_x_side = jnp.zeros((TILE, 128), F32)
        for v in range(2):
            views = pl.ds(v * TILE, TILE)
            m = natural(bands(v, plane, 1, False))
            put(fwd_y, (plane, slice(None), views), m[:, 128:384].T)
            put(back_y, (plane, v), m[:, 128:384])
            low, high = m[:, 0:128].T[120:128] * has_low_y, m[:, 384:512].T[0:8] * has_high_y
            nothing = jnp.zeros((8, TILE), F32)
            put(
                fwd_y_halo,
                (plane, slice(None), views),
                jnp.concatenate([low, nothing, high, nothing], axis=0),
            )
            m = natural(bands(v, plane, 1, True))
            low, high = m[:, 0:128].T[120:128] * has_low_y, m[:, 384:512].T[0:8] * has_high_y
            both = [low, nothing, high, nothing] if v == 0 else [nothing, low, nothing, high]
            put(back_y_halo, (plane, v), jnp.concatenate(both, axis=0))
            m = reordered(bands(v, plane, 0, False))
            put(fwd_x, (plane, v), m[:, 128:384])
            put(back_x, (plane, v), m[:, 128:384].T)
            low = pltpu.roll(m[:, 0:128], 8, 1) * has_low_x
            high = pltpu.roll(m[:, 384:512], 16, 1) * has_high_x
            side = jnp.where(lane < 8, low, jnp.where((lane >= 16) & (lane < 24), high, 0.0))
            put(fwd_x_halo, (plane, v), side[:, :32])
            m = natural(bands(v, plane, 0, True))
            low = pltpu.roll(m[:, 0:128], 8 + 8 * v, 1) * has_low_x
            high = pltpu.roll(m[:, 384:512], 16 + 8 * v, 1) * has_high_x
            first = 8 * v
            back_x_side = jnp.where(
                (lane >= first) & (lane < first + 8),
                low,
                jnp.where((lane >= first + 16) & (lane < first + 24), high, back_x_side),
            )
        put(back_x_halo, (plane,), back_x_side[:, :32])

    def forward(field, exchange, plane):
        rows, columns = read_halo(exchange, plane)
        tall = jnp.concatenate([field.astype(BF16), rows], axis=0)
        along_y = (
            dot(tall, fwd_y[0, plane])
            + dot(tall, fwd_y[1, plane])
            + dot(columns, fwd_y_halo[0, plane])
            + dot(columns, fwd_y_halo[1, plane])
        ).astype(BF16)
        blurred = []
        for v in range(2):
            mine = along_y[:, v * TILE : (v + 1) * TILE]
            main, side = mine[:TILE], mine[TILE:]
            blurred.append(
                dot(fwd_x[0, plane, v], main)
                + dot(fwd_x[1, plane, v], main)
                + dot(fwd_x_halo[0, plane, v], side)
                + dot(fwd_x_halo[1, plane, v], side)
                + background[v, plane]
            )
        return blurred

    def correction(exchange, plane):
        rows, columns = read_halo(exchange, plane)
        total = jnp.zeros((TILE, TILE), F32)
        sides = []
        for v in range(2):
            here_ratio = jnp.concatenate([ratio[v, 0], ratio[v, 1]], axis=1)
            tall = jnp.concatenate([here_ratio.astype(BF16), rows], axis=0)
            along_y = (
                dot(tall, back_y[0, plane, v])
                + dot(tall, back_y[1, plane, v])
                + dot(columns, back_y_halo[0, plane, v])
                + dot(columns, back_y_halo[1, plane, v])
            )
            high, low = split(along_y[:TILE])
            total = (
                total
                + dot(back_x[0, plane, v], high)
                + dot(back_x[0, plane, v], low)
                + dot(back_x[1, plane, v], high)
            )
            sides.append(along_y[TILE:])
        view = (iota((32, TILE), 0) // 8) % 2
        high, low = split(jnp.where(view == 0, sides[0], sides[1]))
        return (
            total
            + dot(back_x_halo[0, plane], high)
            + dot(back_x_halo[0, plane], low)
            + dot(back_x_halo[1, plane], high)
        )

    for plane in range(2):
        wait_halo(0, plane)
        for v, blurred in enumerate(forward(estimate[plane], 0, plane)):
            inverse[plane, v] = 1.0 / blurred

    rest = ids_in.at[pl.ds(1, DEVICES - 1)]
    pltpu.make_async_copy(rest, rest, ids_here).wait()
    ids_in[pl.ds(0, 1)] = ids_out[pl.ds(0, 1)]
    spot = iota((512, 256), 0).astype(F32)
    picked = (iota((8, 128), 1) // 16) == iota((8, 128), 0)
    for group in range(GROUPS):
        halves = []
        for half in range(2):
            eight = ids_in[pl.ds(group * GROUP + half * 8, 8)].reshape(8, 128)
            halves.append(jnp.sum(jnp.where(picked, eight, 0.0), axis=0, keepdims=True))
        wanted = jnp.concatenate(halves, axis=1)
        landing[:, pl.ds(group * 256, 256)] = jnp.where(spot == wanted, 1.0, 0.0).astype(BF16)

    def land(plane):
        incoming[plane, pl.ds(0, 16)] = outgoing[plane, pl.ds(0, 16)]
        for group in range(GROUPS):
            first = group * 256
            came = (
                incoming.at[plane, pl.ds(16, 240)]
                if group == 0
                else incoming.at[plane, pl.ds(first, 256)]
            )
            pltpu.make_async_copy(came, came, data_here.at[plane, group]).wait()
            part = dot(
                landing[:, pl.ds(first, 256)], incoming[plane, pl.ds(first, 256), :]
            )
            summed[...] = part if group == 0 else summed[...] + part
        group_of = iota((32, 128), 1) // 32
        for v in range(2):
            for h in range(2):
                for wide in range(2):
                    source = [
                        summed[
                            pl.ds(v * 256 + (wide * 4 + by) * 32, 32), pl.ds(h * 128, 128)
                        ]
                        for by in range(4)
                    ]
                    for x4 in range(4):
                        tile = source[x4]
                        for by in range(4):
                            if by != x4:
                                moved = pltpu.roll(source[by], ((by - x4) % 4) * 32, 1)
                                tile = jnp.where(group_of == by, moved, tile)
                        measured[
                            v, pl.ds((h * 4 + x4) * 32, 32), pl.ds(wide * 128, 128)
                        ] = tile

    def put_ratio(v, value):
        ratio[v, 0] = value[:, :128]
        ratio[v, 1] = value[:, 128:]

    for plane in range(2):
        land(plane)
        for v in range(2):
            put_ratio(v, measured[v] * inverse[plane, v])
        pack_halo([ratio.at[0], ratio.at[1]], False, 1, plane)
        send_halo(1, plane)
        wait_halo(1, plane)
        result[plane] = estimate[plane] * (0.5 * correction(1, plane))
        pack_halo([result.at[plane]], True, 2, plane)
        send_halo(2, plane)
        wait_halo(2, plane)
        for v, blurred in enumerate(forward(result[plane], 2, plane)):
            put_ratio(v, measured[v] / blurred)
        pack_halo([ratio.at[0], ratio.at[1]], False, 3, plane)
        send_halo(3, plane)
        wait_halo(3, plane)
        result[plane] = result[plane] * (0.5 * correction(3, plane))

    rest = ids_out.at[pl.ds(1, DEVICES - 1)]
    pltpu.make_async_copy(rest, rest, ids_sent).wait()
    for plane in range(2):
        rest = outgoing.at[plane, pl.ds(16, (DEVICES - 1) * 16)]
        pltpu.make_async_copy(rest, rest, data_sent.at[plane]).wait()
        for exchange in range(4):
            whole = halo_out.at[exchange, plane]
            pltpu.make_async_copy(whole, whole, halo_sent.at[exchange, plane]).wait()


def shards(blocks, owner_route, block_slot, estimate, background, psf_taps, psf_index):
    owners = owner_route.reshape(owner_route.shape[:2])
    vmem = pl.BlockSpec(memory_space=pltpu.VMEM)
    smem = pl.BlockSpec(memory_space=pltpu.SMEM)
    dma = pltpu.SemaphoreType.DMA
    return pl.pallas_call(
        kernel,
        out_shape=jax.ShapeDtypeStruct(estimate.shape, F32),
        in_specs=[vmem, vmem, vmem, vmem, smem, smem, smem],
        out_specs=vmem,
        scratch_shapes=[
            pltpu.VMEM((2, 1024, 256), BF16),
            pltpu.VMEM((2, DEVICES * 16, 256), BF16),
            pltpu.VMEM((2, DEVICES * 16, 256), BF16),
            pltpu.VMEM((DEVICES, 1, 128), F32),
            pltpu.VMEM((DEVICES, 1, 128), F32),
            pltpu.VMEM((512, DEVICES * 16), BF16),
            pltpu.VMEM((512, 256), F32),
            pltpu.VMEM((2, TILE, TILE), F32),
            pltpu.VMEM((2, 2, TILE, TILE), F32),
            pltpu.VMEM((2, 2, TILE, 128), F32),
            pltpu.VMEM((4, TILE, 128), F32),
            pltpu.VMEM((4, 2, HALO_ROWS, 128), BF16),
            pltpu.VMEM((4, 2, HALO_ROWS, 128), BF16),
            pltpu.VMEM((2, 2, TILE, 2 * TILE), BF16),
            pltpu.VMEM((2, 2, 32, 2 * TILE), BF16),
            pltpu.VMEM((2, 2, 2, TILE, TILE), BF16),
            pltpu.VMEM((2, 2, 2, TILE, 32), BF16),
            pltpu.VMEM((2, 2, 2, TILE, TILE), BF16),
            pltpu.VMEM((2, 2, 2, 32, TILE), BF16),
            pltpu.VMEM((2, 2, 2, TILE, TILE), BF16),
            pltpu.VMEM((2, 2, TILE, 32), BF16),
            pltpu.SemaphoreType.REGULAR,
            dma((2,)),
            dma((2, GROUPS)),
            dma,
            dma,
            dma((4, 2)),
            dma((4, 2)),
        ],
        compiler_params=pltpu.CompilerParams(
            collective_id=0, has_side_effects=True, vmem_limit_bytes=48 << 20
        ),
        cost_estimate=pl.CostEstimate(
            flops=8_000_000_000, bytes_accessed=2 << 20, transcendentals=0
        ),
    )(blocks, owners, block_slot, estimate, background, psf_taps, psf_index)


def solution(mesh):
    return jax.shard_map(
        shards,
        mesh=mesh,
        in_specs=(
            P(None, ("gx", "gy"), None),
            P(None, ("gx", "gy"), None),
            P(None, ("gx", "gy")),
            P(None, "gx", "gy"),
            P(),
            P(),
            P(),
        ),
        out_specs=P(None, "gx", "gy"),
        check_vma=False,
    )
```

profile of v0, /device:TPU:0, one launch (start us, length us, event | category | flops | bytes accessed | tf_op | source)
XLA Modules:
  0.0 91.6 jit_solution(11042486047170949232)
XLA Ops:
  0.0 0.0 copy-start.3
  0.0 0.7 copy-done.3
  0.7 0.0 copy-start
  0.7 1.2 %copy-done = bf16[2,128,2048]{2,1,0:T(8,128)(2,1)S(1)} copy-done((bf16[2,128,2048]{2,1,0:T(8,128)(2,1)S(1)}, bf16[2,128,2048]{2,1,0:T(8,128)(2,1)}, u32[]{:S(2)}) %copy-start) | copy-done | bytes 1048600
  1.9 0.0 copy-start.1
  1.9 1.0 %copy-done.1 = f32[2,256,256]{2,1,0:T(8,128)S(1)} copy-done((f32[2,256,256]{2,1,0:T(8,128)S(1)}, f32[2,256,256]{2,1,0:T(8,128)}, u32[]{:S(2)}) %copy-start.1) | copy-done | bytes 524312
  2.9 0.0 copy-start.2
  2.9 0.7 copy-done.2
  3.6 0.0 copy-start.4
  3.6 0.7 copy-done.4
  4.3 0.0 copy-start.5
  4.3 0.7 copy-done.5
  5.0 0.0 copy-start.6
  5.0 0.7 copy-done.6
  5.7 85.1 %shard_map.73 = f32[2,256,256]{2,1,0:T(8,128)S(1)} custom-call(bf16[2,128,2048]{2,1,0:T(8,128)(2,1)S(1)} %copy-done, s32[2,128]{1,0:T(2,128)S(1)} %bitcast.1, s32[2,128]{1,0:T(2,128)S(1)} %copy-done.4, f32[2,256,256]{2,1,0:T(8,128)S(1)} %copy-done.1, f32[2,2]{1,0:T(2,128)S(1)} %copy-done.5, f32[2,4,2,17]{3,2,1,0:T(2,128)S(1)} %copy-done.2, s32[2,2]{1,0:T(2,128)S(1)} %copy-done.6), custom_call_target="tpu_custom_call" | custom-call | flops 8000000000 | bytes 2097152 | tf_op jit(solution)/shard_map/pallas_call | solution.py:542
  90.8 0.8 copy.9
Async XLA Ops:
  0.0 0.7 copy-start.3
  0.7 1.2 %copy-start = (bf16[2,128,2048]{2,1,0:T(8,128)(2,1)S(1)}, bf16[2,128,2048]{2,1,0:T(8,128)(2,1)}, u32[]{:S(2)}) copy-start(bf16[2,128,2048]{2,1,0:T(8,128)(2,1)} %blocks.1) | copy-start | bytes 3145732
  1.9 1.0 %copy-start.1 = (f32[2,256,256]{2,1,0:T(8,128)S(1)}, f32[2,256,256]{2,1,0:T(8,128)}, u32[]{:S(2)}) copy-start(f32[2,256,256]{2,1,0:T(8,128)} %estimate.1) | copy-start | bytes 1572868
  2.9 0.7 copy-start.2
  3.6 0.7 copy-start.4
  4.3 0.7 copy-start.5
  5.0 0.7 copy-start.6
where the time goes:
time: 91.9 us; the launch traced here: 91.6 us
  Pallas kernels  85.1 us (93%)
  local copies, waits for them, and re-layouts  6.47 us (7%)
    pallas_call x1, Pallas kernels, shards(): pl.pallas_call(kernel, out_shape=jax.ShapeDtypeStruct(estimate.shape, F32...  85.1 us
    unnamed x15, local copies, waits for them, and re-layouts  6.47 us

commit v1 on v0

v1 whole, which is shorter than its diff:
```python
import jax
import jax.numpy as jnp
from jax import lax
from jax.experimental import pallas as pl
from jax.experimental.pallas import tpu as pltpu
from jax.sharding import PartitionSpec as P

MESH = pl.DeviceIdType.MESH
F32 = jnp.float32
BF16 = jnp.bfloat16

N_GX, N_GY = 16, 8
DEVICES = N_GX * N_GY
TILE = 256
TAPS = 17
WIDE = TILE + 64
LANES = 384
STEP, STEP_INVERSE = 27, 19
GROUP = 16
GROUPS = DEVICES // GROUP
EARLY = 2
ESTIMATE_PARTS = (
    (0, 64, 1, 0),
    (64, 64, -1, 0),
    (128, 64, 0, 1),
    (192, 64, 0, -1),
    (256, 32, 1, 1),
    (288, 32, 1, -1),
    (320, 32, -1, 1),
    (352, 32, -1, -1),
)
ESTIMATE_ROWS = 384
SIDE_PARTS = ((256, 128, 0, 1), (384, 128, 0, -1))
OTHER_PARTS = (
    (0, 128, 1, 0),
    (128, 128, -1, 0),
    (512, 32, 1, 1),
    (544, 32, 1, -1),
    (576, 32, -1, 1),
    (608, 32, -1, -1),
)
MEASURED_ROWS = 640


def iota(shape, dim):
    return lax.broadcasted_iota(jnp.int32, shape, dim)


def dot(a, b):
    return jnp.dot(a, b, preferred_element_type=F32)


def split(a):
    high = a.astype(BF16)
    return high, (a - high.astype(F32)).astype(BF16)


def torus_position():
    gx, gy = lax.axis_index("gx"), lax.axis_index("gy")
    return gy // 2, ((gx // 2) % 2) * 2 + gy % 2, gx // 4, gx % 2


def partner(slot, here):
    x, y, z, core = here
    shift = (slot * STEP) % DEVICES
    core = (core + shift % 2) % 2
    x = (x + (shift // 2) % 4) % 4
    y = (y + (shift // 8) % 4) % 4
    z = (z + shift // 32) % 4
    return z * 4 + (y // 2) * 2 + core, x * 2 + y % 2


def slot_of(tile, here):
    x, y, z, core = here
    gx, gy = tile >> 3, tile & 7
    d_core = ((gx & 1) - core) & 1
    dx = ((gy >> 1) - x) & 3
    dy = ((((gx >> 1) & 1) * 2 + (gy & 1)) - y) & 3
    dz = ((gx >> 2) - z) & 3
    return ((d_core + 2 * dx + 8 * dy + 32 * dz) * STEP_INVERSE) & (DEVICES - 1)


def kernel(
    blocks_in,
    owners_in,
    places_in,
    estimate_in,
    background_in,
    taps_in,
    index_in,
    result,
    blocks,
    owners,
    places,
    estimate,
    background,
    psf_taps,
    psf_index,
    staged,
    outgoing,
    incoming,
    ids_out,
    ids_in,
    landing,
    summed,
    wide_estimate,
    measured,
    inverse,
    final,
    shuffle,
    estimate_out,
    estimate_halo,
    measured_out,
    measured_halo,
    fwd_y,
    fwd_x,
    back_y,
    back_x,
    ready,
    loaded,
    stored,
    data_sent,
    data_here,
    ids_sent,
    ids_here,
    estimate_sent,
    estimate_here,
    measured_sent,
    measured_here,
):
    gx, gy = lax.axis_index("gx"), lax.axis_index("gy")
    here = torus_position()
    barrier = pltpu.get_barrier_semaphore()

    loads = [
        pltpu.make_async_copy(source, target, loaded.at[i])
        for i, (source, target) in enumerate(
            (
                (owners_in, owners),
                (places_in, places),
                (estimate_in, estimate),
                (blocks_in, blocks),
                (background_in, background),
                (taps_in, psf_taps),
                (index_in, psf_index),
            )
        )
    ]
    for load in loads:
        load.start()

    for step in range(1, N_GX):
        pl.semaphore_signal(
            barrier, inc=1, device_id=((gx + step) % N_GX, gy), device_id_type=MESH
        )
    for step in range(1, N_GY):
        pl.semaphore_signal(
            barrier, inc=1, device_id=(gx, (gy + step) % N_GY), device_id_type=MESH
        )

    has_low_x = jnp.where(gx > 0, 1.0, 0.0)
    has_high_x = jnp.where(gx < N_GX - 1, 1.0, 0.0)
    has_low_y = jnp.where(gy > 0, 1.0, 0.0)
    has_high_y = jnp.where(gy < N_GY - 1, 1.0, 0.0)
    narrow = iota((32, 128), 1)

    def turn(a, shift):
        return pltpu.roll(a, shift % 128, 1) if shift % 128 else a

    def sides(low, high):
        at = iota(low.shape, 1)
        return jnp.where(
            at < 32, low * has_low_y, jnp.where(at < 64, high * has_high_y, 0.0)
        )

    def send_parts(parts, out, into, sent, arrived):
        for start, rows, to_x, to_y in parts:
            pltpu.make_async_remote_copy(
                src_ref=out.at[pl.ds(start, rows)],
                dst_ref=into.at[pl.ds(start, rows)],
                send_sem=sent,
                recv_sem=arrived,
                device_id=((gx + to_x + N_GX) % N_GX, (gy + to_y + N_GY) % N_GY),
                device_id_type=MESH,
            ).start()

    def pack_estimate(plane):
        out = estimate_out.at[plane]
        for at, row in ((0, 224), (64, 0)):
            for tile in range(2):
                out[pl.ds(at + 32 * tile, 32)] = estimate[
                    plane, pl.ds(row, 32), pl.ds(128 * tile, 128)
                ].astype(BF16)
        for at, tile in ((128, 1), (192, 0)):
            packed = jnp.zeros((64, 128), F32)
            for slab in range(4):
                piece = estimate[plane, pl.ds(64 * slab, 64), pl.ds(128 * tile, 128)]
                moved = turn(piece, 32 * slab + 32 * tile)
                packed = jnp.where(iota((64, 128), 1) // 32 == slab, moved, packed)
            out[pl.ds(at, 64)] = packed.astype(BF16)
        for at, row, tile in ((256, 224, 1), (288, 224, 0), (320, 0, 1), (352, 0, 0)):
            out[pl.ds(at, 32)] = estimate[
                plane, pl.ds(row, 32), pl.ds(128 * tile, 128)
            ].astype(BF16)

    def widen_estimate(plane):
        whole = estimate_halo.at[plane]
        pltpu.make_async_copy(whole, whole, estimate_here.at[plane]).wait()

        def got(start, rows):
            return estimate_halo[plane, pl.ds(start, rows)].astype(F32)

        wide = wide_estimate.at[plane]
        wide[pl.ds(0, TILE), pl.ds(0, TILE)] = estimate[plane]
        for slab in range(4):
            wide[pl.ds(64 * slab, 64), pl.ds(TILE, 128)] = sides(
                turn(got(128, 64), -32 * slab), turn(got(192, 64), 32 - 32 * slab)
            )
        for row, start, corner, there in (
            (TILE, 0, 256, has_low_x),
            (TILE + 32, 64, 320, has_high_x),
        ):
            for tile in range(2):
                wide[pl.ds(row, 32), pl.ds(128 * tile, 128)] = (
                    got(start + 32 * tile, 32) * there
                )
            wide[pl.ds(row, 32), pl.ds(TILE, 128)] = (
                sides(turn(got(corner, 32), 32), turn(got(corner + 32, 32), 32)) * there
            )

    def send_sides(plane):
        for at, by in ((256, 7), (384, 0)):
            for v in range(2):
                for h in range(2):
                    measured_out[plane, pl.ds(at + 64 * v + 32 * h, 32)] = summed[
                        pl.ds(v * 256 + by * 32, 32), pl.ds(128 * h, 128)
                    ].astype(BF16)
        send_parts(
            SIDE_PARTS,
            measured_out.at[plane],
            measured_halo.at[plane],
            measured_sent.at[plane],
            measured_here.at[plane],
        )

    def send_others(plane):
        out = measured_out.at[plane]

        def edge(v, tile, bx):
            return jnp.concatenate(
                [measured[v, tile, pl.ds(q * 8 + bx, 8, stride=32), :] for q in range(4)], axis=0
            )

        for at, bx, corner in ((0, 7, 512), (128, 0, 576)):
            for tile in range(2):
                edges = [edge(v, tile, bx) for v in range(2)]
                for v in range(2):
                    out[pl.ds(at + 64 * v + 32 * tile, 32)] = edges[v].astype(BF16)
                if tile == 1:
                    both = jnp.where(narrow >= 96, edges[0], turn(edges[1], 96))
                    out[pl.ds(corner, 32)] = both.astype(BF16)
                else:
                    both = jnp.where(narrow < 32, edges[0], turn(edges[1], 32))
                    out[pl.ds(corner + 32, 32)] = both.astype(BF16)
        send_parts(
            OTHER_PARTS,
            measured_out.at[plane],
            measured_halo.at[plane],
            measured_sent.at[plane],
            measured_here.at[plane],
        )

    def widen_measured(plane):
        whole = measured_halo.at[plane]
        pltpu.make_async_copy(whole, whole, measured_here.at[plane]).wait()

        def got(start):
            return measured_halo[plane, pl.ds(start, 32)].astype(F32)

        for v in range(2):
            for x8 in range(8):
                at, back = 64 * v + 32 * (x8 // 4), -32 * (x8 % 4)
                measured[v, 2, pl.ds(32 * x8, 32), :] = sides(
                    turn(got(256 + at), back), turn(got(384 + at), back + 32)
                )
            for row, start, corner, there in (
                (TILE, 0, 512, has_low_x),
                (TILE + 32, 128, 576, has_high_x),
            ):
                for tile in range(2):
                    measured[v, tile, pl.ds(row, 32), :] = (
                        got(start + 64 * v + 32 * tile) * there
                    )
                measured[v, 2, pl.ds(row, 32), :] = (
                    sides(
                        turn(got(corner), 32 + 32 * v), turn(got(corner + 32), 32 - 32 * v)
                    )
                    * there
                )

    loads[0].wait()
    loads[1].wait()
    slot_rows, rank_rows, rank_columns, place_columns = [], [], [], []
    sub, lane = iota((128, 128), 0), iota((128, 128), 1)
    for v in range(2):
        row = slot_of(owners[pl.ds(v, 1), :], here)
        across = jnp.broadcast_to(row, (128, 128))
        same = across == across.T
        slot_rows.append(row)
        rank_rows.append(
            jnp.sum(jnp.where(same & (sub < lane), 1.0, 0.0), axis=0, keepdims=True).astype(
                jnp.int32
            )
        )
        rank_columns.append(
            jnp.sum(jnp.where(same & (lane < sub), 1.0, 0.0), axis=1, keepdims=True)
        )
        place = places[pl.ds(v, 1), :]
        spot = ((place & 7) * 32 + (place >> 3) + 1).astype(F32)
        place_columns.append(jnp.broadcast_to(spot, (128, 128)).T)

    lane_view, lane_rank, lane_part = (lane >> 3) & 1, (lane >> 2) & 1, lane & 3
    ids = jnp.zeros((128, 128), F32)
    for v in range(2):
        taken = jnp.where(sub == slot_rows[v], 1.0, 0.0).astype(BF16)
        mine = (lane_view == v) & (lane_rank.astype(F32) == rank_columns[v])
        ids = ids + dot(taken, jnp.where(mine, place_columns[v], 0.0).astype(BF16))
    ids = jnp.where(ids > 0.0, ids + (lane_view * 256 + lane_part * 8 - 1).astype(F32), -1.0)
    ids_out[...] = ids.reshape(128, 1, 128)

    target = jnp.concatenate(
        [
            slot_rows[v] * 16 + v * 8 + rank_rows[v] * 4 + part
            for v in range(2)
            for part in range(4)
        ],
        axis=1,
    )
    loads[3].wait()
    for plane in range(2):
        for v in range(2):
            for part in range(4):
                staged[plane, pl.ds((v * 4 + part) * 128, 128), :] = blocks[
                    v, :, pl.ds(plane * 1024 + part * 256, 256)
                ]
    loads[2].wait()
    for plane in range(2):
        pack_estimate(plane)

    pl.semaphore_wait(barrier, N_GX + N_GY - 2)
    for step in range(1, N_GY):
        pl.semaphore_signal(
            ready, inc=1, device_id=(gx, (gy + step) % N_GY), device_id_type=MESH
        )
    pl.semaphore_wait(ready, N_GY - 1)

    for plane in range(2):
        send_parts(
            ESTIMATE_PARTS,
            estimate_out.at[plane],
            estimate_halo.at[plane],
            estimate_sent.at[plane],
            estimate_here.at[plane],
        )

    def id_copy(slot):
        return pltpu.make_async_remote_copy(
            src_ref=ids_out.at[pl.ds(slot, 1)],
            dst_ref=ids_in.at[pl.ds(slot, 1)],
            send_sem=ids_sent,
            recv_sem=ids_here,
            device_id=partner(slot, here),
            device_id_type=MESH,
        )

    def data_copy(plane, slot):
        rows = pl.ds(pl.multiple_of(slot * 16, 16), 16)
        return pltpu.make_async_remote_copy(
            src_ref=outgoing.at[plane, rows],
            dst_ref=incoming.at[plane, rows],
            send_sem=data_sent.at[plane],
            recv_sem=data_here.at[plane, slot // GROUP],
            device_id=partner(slot, here),
            device_id_type=MESH,
        )

    @pl.loop(1, DEVICES)
    def _(slot):
        id_copy(slot).start()

    def pick_group(plane, group):
        rows = GROUP * 16
        wanted = iota((rows, 1024), 0) + group * rows
        pick = jnp.where(wanted == target, 1.0, 0.0).astype(BF16)
        outgoing[plane, pl.ds(pl.multiple_of(group * rows, rows), rows), :] = dot(
            pick, staged[plane]
        ).astype(BF16)

    def send_group(plane, group):
        for j in range(GROUP):
            if j == 0:

                @pl.when(group > 0)
                def _():
                    data_copy(plane, group * GROUP).start()

            else:
                data_copy(plane, group * GROUP + j).start()

    @pl.loop(0, GROUPS)
    def _(group):
        pick_group(0, group)
        send_group(0, group)

    @pl.loop(0, GROUPS)
    def _(group):
        pick_group(1, group)

        @pl.when(group < EARLY)
        def _():
            send_group(1, group)

    for load in loads[4:]:
        load.wait()

    def bands(v, plane, axis, reverse):
        kernel_index = psf_index[v, plane]
        wide = iota((8, 512), 1)
        taps = jnp.zeros((8, 512), F32)
        total = jnp.zeros((8, 512), F32)
        for t in range(TAPS):
            value = psf_taps[v, kernel_index, axis, t]
            at = 88 + (TAPS - 1 - t if reverse else t)
            taps = jnp.where(wide == at, value, taps)
            total = total + value
        rows = jnp.broadcast_to((taps / total)[0:1], (WIDE, 512))
        return pltpu.roll(rows, 0, 1, stride=1, stride_axis=0)

    def by_lanes(m):
        at = iota((m.shape[0], 128), 1)
        side = jnp.where(
            at < 32, turn(m[:, :128], 32), jnp.where(at < 64, turn(m[:, 384:], 32), 0.0)
        )
        return jnp.concatenate([m[:, 128:384], side], axis=1)

    def by_rows(m):
        return jnp.concatenate([m[32 : 32 + TILE], m[:32], m[32 + TILE :]], axis=0)

    def reordered(m):
        for tile in range(4):
            shuffle[tile] = m[:, tile * 128 : (tile + 1) * 128]
        main = [
            jnp.concatenate(
                [
                    shuffle[tile, pl.ds(32 + q * 8 + x8, 8, stride=32), :]
                    for tile in range(4)
                ],
                axis=1,
            )
            for x8 in range(8)
            for q in range(4)
        ]
        return jnp.concatenate(main + [m[:32], m[32 + TILE :]], axis=0)

    def put(ref, index, value):
        high, low = split(value)
        ref[(0,) + index] = high
        ref[(1,) + index] = low

    for plane in range(2):
        for v in range(2):
            m = by_lanes(by_rows(bands(v, plane, 1, True)))
            put(fwd_y, (plane, slice(None), pl.ds(v * LANES, LANES)), m)
            put(back_y, (plane, v), by_lanes(by_rows(bands(v, plane, 1, False))))
            m = by_lanes(reordered(bands(v, plane, 0, False)))
            put(fwd_x, (plane, v), m[:, :WIDE])
            square = jnp.concatenate([m, jnp.zeros((LANES - WIDE, LANES), F32)], axis=0)
            put(back_x, (plane, v), square.T[:WIDE, :WIDE])

    def forward(field, plane):
        field = field.astype(BF16)[:, :WIDE]
        along_y = (dot(field, fwd_y[0, plane]) + dot(field, fwd_y[1, plane])).astype(BF16)
        blurred = []
        for v in range(2):
            mine = along_y[:, v * LANES : (v + 1) * LANES]
            blurred.append(
                dot(fwd_x[0, plane, v], mine)
                + dot(fwd_x[1, plane, v], mine)
                + background[v, plane]
            )
        return blurred

    def correction(ratios, plane, rows, lanes):
        total = jnp.zeros((rows, lanes), F32)
        for v in range(2):
            ratio = ratios[v].astype(BF16)[:, :WIDE]
            high, low = split(
                dot(ratio, back_y[0, plane, v][:, :lanes])
                + dot(ratio, back_y[1, plane, v][:, :lanes])
            )
            total = (
                total
                + dot(back_x[0, plane, v][:rows], high)
                + dot(back_x[0, plane, v][:rows], low)
                + dot(back_x[1, plane, v][:rows], high)
            )
        return total

    for plane in range(2):
        widen_estimate(plane)
        for v, blurred in enumerate(forward(wide_estimate[plane], plane)):
            inverse[plane, v] = 1.0 / blurred

    rest = ids_in.at[pl.ds(1, DEVICES - 1)]
    pltpu.make_async_copy(rest, rest, ids_here).wait()
    ids_in[pl.ds(0, 1)] = ids_out[pl.ds(0, 1)]
    spot = iota((512, 256), 0).astype(F32)
    picked = (iota((8, 128), 1) // 16) == iota((8, 128), 0)
    for group in range(GROUPS):
        halves = []
        for half in range(2):
            eight = ids_in[pl.ds(group * GROUP + half * 8, 8)].reshape(8, 128)
            halves.append(jnp.sum(jnp.where(picked, eight, 0.0), axis=0, keepdims=True))
        wanted = jnp.concatenate(halves, axis=1)
        landing[:, pl.ds(group * 256, 256)] = jnp.where(spot == wanted, 1.0, 0.0).astype(BF16)

    def land(plane):
        incoming[plane, pl.ds(0, 16)] = outgoing[plane, pl.ds(0, 16)]
        for group in range(GROUPS):
            first = group * 256
            came = (
                incoming.at[plane, pl.ds(16, 240)]
                if group == 0
                else incoming.at[plane, pl.ds(first, 256)]
            )
            pltpu.make_async_copy(came, came, data_here.at[plane, group]).wait()
            part = dot(
                landing[:, pl.ds(first, 256)], incoming[plane, pl.ds(first, 256), :]
            )
            summed[...] = part if group == 0 else summed[...] + part
        send_sides(plane)
        group_of = narrow // 32
        for v in range(2):
            for h in range(2):
                for wide in range(2):
                    source = [
                        summed[
                            pl.ds(v * 256 + (wide * 4 + by) * 32, 32), pl.ds(h * 128, 128)
                        ]
                        for by in range(4)
                    ]
                    for x4 in range(4):
                        tile = source[x4]
                        for by in range(4):
                            if by != x4:
                                moved = pltpu.roll(source[by], ((by - x4) % 4) * 32, 1)
                                tile = jnp.where(group_of == by, moved, tile)
                        measured[v, wide, pl.ds((h * 4 + x4) * 32, 32), :] = tile

    def wide_measured(v):
        return jnp.concatenate([measured[v, tile] for tile in range(3)], axis=1)

    def store(plane):
        return pltpu.make_async_copy(final.at[plane], result.at[plane], stored.at[plane])

    for plane in range(2):
        land(plane)
        send_others(plane)
        if plane == 0:

            @pl.loop(EARLY, GROUPS)
            def _(group):
                send_group(1, group)

        widen_measured(plane)
        ratios = [wide_measured(v) * inverse[plane, v] for v in range(2)]
        current = wide_estimate[plane] * (0.5 * correction(ratios, plane, WIDE, LANES))
        ratios = [
            wide_measured(v) / blurred for v, blurred in enumerate(forward(current, plane))
        ]
        final[plane] = current[:TILE, :TILE] * (
            0.5 * correction(ratios, plane, TILE, TILE)
        )
        store(plane).start()

    rest = ids_out.at[pl.ds(1, DEVICES - 1)]
    pltpu.make_async_copy(rest, rest, ids_sent).wait()
    for plane in range(2):
        rest = outgoing.at[plane, pl.ds(16, (DEVICES - 1) * 16)]
        pltpu.make_async_copy(rest, rest, data_sent.at[plane]).wait()
        whole = estimate_out.at[plane]
        pltpu.make_async_copy(whole, whole, estimate_sent.at[plane]).wait()
        whole = measured_out.at[plane]
        pltpu.make_async_copy(whole, whole, measured_sent.at[plane]).wait()
        store(plane).wait()


def shards(blocks, owner_route, block_slot, estimate, background, psf_taps, psf_index):
    owners = owner_route.reshape(owner_route.shape[:2])
    anywhere = pl.BlockSpec(memory_space=pl.ANY)
    dma = pltpu.SemaphoreType.DMA
    return pl.pallas_call(
        kernel,
        out_shape=jax.ShapeDtypeStruct(estimate.shape, F32),
        in_specs=[anywhere] * 7,
        out_specs=anywhere,
        scratch_shapes=[
            pltpu.VMEM(blocks.shape, BF16),
            pltpu.VMEM(owners.shape, jnp.int32),
            pltpu.VMEM(block_slot.shape, jnp.int32),
            pltpu.VMEM(estimate.shape, F32),
            pltpu.SMEM(background.shape, F32),
            pltpu.SMEM(psf_taps.shape, F32),
            pltpu.SMEM(psf_index.shape, jnp.int32),
            pltpu.VMEM((2, 1024, 256), BF16),
            pltpu.VMEM((2, DEVICES * 16, 256), BF16),
            pltpu.VMEM((2, DEVICES * 16, 256), BF16),
            pltpu.VMEM((DEVICES, 1, 128), F32),
            pltpu.VMEM((DEVICES, 1, 128), F32),
            pltpu.VMEM((512, DEVICES * 16), BF16),
            pltpu.VMEM((512, 256), F32),
            pltpu.VMEM((2, WIDE, LANES), F32),
            pltpu.VMEM((2, 3, WIDE, 128), F32),
            pltpu.VMEM((2, 2, WIDE, LANES), F32),
            pltpu.VMEM((2, TILE, TILE), F32),
            pltpu.VMEM((4, WIDE, 128), F32),
            pltpu.VMEM((2, ESTIMATE_ROWS, 128), BF16),
            pltpu.VMEM((2, ESTIMATE_ROWS, 128), BF16),
            pltpu.VMEM((2, MEASURED_ROWS, 128), BF16),
            pltpu.VMEM((2, MEASURED_ROWS, 128), BF16),
            pltpu.VMEM((2, 2, WIDE, 2 * LANES), BF16),
            pltpu.VMEM((2, 2, 2, WIDE, WIDE), BF16),
            pltpu.VMEM((2, 2, 2, WIDE, LANES), BF16),
            pltpu.VMEM((2, 2, 2, WIDE, WIDE), BF16),
            pltpu.SemaphoreType.REGULAR,
            dma((7,)),
            dma((2,)),
            dma((2,)),
            dma((2, GROUPS)),
            dma,
            dma,
            dma((2,)),
            dma((2,)),
            dma((2,)),
            dma((2,)),
        ],
        compiler_params=pltpu.CompilerParams(
            collective_id=0, has_side_effects=True, vmem_limit_bytes=48 << 20
        ),
        cost_estimate=pl.CostEstimate(
            flops=8_000_000_000, bytes_accessed=2 << 20, transcendentals=0
        ),
    )(blocks, owners, block_slot, estimate, background, psf_taps, psf_index)


def solution(mesh):
    return jax.shard_map(
        shards,
        mesh=mesh,
        in_specs=(
            P(None, ("gx", "gy"), None),
            P(None, ("gx", "gy"), None),
            P(None, ("gx", "gy")),
            P(None, "gx", "gy"),
            P(),
            P(),
            P(),
        ),
        out_specs=P(None, "gx", "gy"),
        check_vma=False,
    )
```

time: 91.9 us -> 72 us (0.78)
  Pallas kernels: 85.1 us -> 65.3 us
    pallas_call x1, Pallas kernels: 85.1 us -> 65.3 us  [shards(): pl.pallas_call(kernel, out_shape=jax.ShapeDtypeStruct(estimate.shape, F32...]
where the time goes in v1:
time: 72 us; the launch traced here: 71.7 us
  Pallas kernels  65.3 us (91%)
  local copies, waits for them, and re-layouts  6.47 us (9%)
    pallas_call x1, Pallas kernels, shards(): pl.pallas_call(kernel, out_shape=jax.ShapeDtypeStruct(estimate.shape, F32...  65.3 us
    unnamed x15, local copies, waits for them, and re-layouts  6.47 us

profile of v1, /device:TPU:0, one launch (start us, length us, event | category | flops | bytes accessed | tf_op | source)
XLA Modules:
  0.0 71.7 jit_solution(1460444887875592025)
XLA Ops:
  0.0 0.0 copy-start.3
  0.0 0.7 copy-done.3
  0.7 0.0 copy-start
  0.7 1.2 %copy-done = bf16[2,128,2048]{2,1,0:T(8,128)(2,1)S(1)} copy-done((bf16[2,128,2048]{2,1,0:T(8,128)(2,1)S(1)}, bf16[2,128,2048]{2,1,0:T(8,128)(2,1)}, u32[]{:S(2)}) %copy-start) | copy-done | bytes 1048600
  1.9 0.0 copy-start.1
  1.9 1.0 %copy-done.1 = f32[2,256,256]{2,1,0:T(8,128)S(1)} copy-done((f32[2,256,256]{2,1,0:T(8,128)S(1)}, f32[2,256,256]{2,1,0:T(8,128)}, u32[]{:S(2)}) %copy-start.1) | copy-done | bytes 524312
  2.9 0.0 copy-start.2
  2.9 0.7 copy-done.2
  3.6 0.0 copy-start.4
  3.6 0.7 copy-done.4
  4.3 0.0 copy-start.5
  4.3 0.7 copy-done.5
  5.0 0.0 copy-start.6
  5.0 0.7 copy-done.6
  5.7 65.3 %shard_map.73 = f32[2,256,256]{2,1,0:T(8,128)S(1)} custom-call(bf16[2,128,2048]{2,1,0:T(8,128)(2,1)S(1)} %copy-done, s32[2,128]{1,0:T(2,128)S(1)} %bitcast.1, s32[2,128]{1,0:T(2,128)S(1)} %copy-done.4, f32[2,256,256]{2,1,0:T(8,128)S(1)} %copy-done.1, f32[2,2]{1,0:T(2,128)S(1)} %copy-done.5, f32[2,4,2,17]{3,2,1,0:T(2,128)S(1)} %copy-done.2, s32[2,2]{1,0:T(2,128)S(1)} %copy-done.6), custom_call_target="tpu_custom_call" | custom-call | flops 8000000000 | bytes 2097152 | tf_op jit(solution)/shard_map/pallas_call | solution.py:602
  70.9 0.8 %copy.9 = f32[2,256,256]{2,1,0:T(8,128)} copy(f32[2,256,256]{2,1,0:T(8,128)S(1)} %shard_map.73) | data formatting | bytes 1048576
Async XLA Ops:
  0.0 0.7 copy-start.3
  0.7 1.2 %copy-start = (bf16[2,128,2048]{2,1,0:T(8,128)(2,1)S(1)}, bf16[2,128,2048]{2,1,0:T(8,128)(2,1)}, u32[]{:S(2)}) copy-start(bf16[2,128,2048]{2,1,0:T(8,128)(2,1)} %blocks_in.1) | copy-start | bytes 3145732
  1.9 1.0 %copy-start.1 = (f32[2,256,256]{2,1,0:T(8,128)S(1)}, f32[2,256,256]{2,1,0:T(8,128)}, u32[]{:S(2)}) copy-start(f32[2,256,256]{2,1,0:T(8,128)} %estimate_in.1) | copy-start | bytes 1572868
  2.9 0.7 copy-start.2
  3.6 0.7 copy-start.4
  4.3 0.7 copy-start.5
  5.0 0.7 copy-start.6

commit v2 on v1

--- a/solution.py
+++ b/solution.py
@@ -18,7 +18,6 @@
 STEP, STEP_INVERSE = 27, 19
 GROUP = 16
 GROUPS = DEVICES // GROUP
-EARLY = 2
 ESTIMATE_PARTS = (
     (0, 64, 1, 0),
     (64, 64, -1, 0),
@@ -106,7 +105,6 @@
     wide_estimate,
     measured,
     inverse,
-    final,
     shuffle,
     estimate_out,
     estimate_halo,
@@ -118,7 +116,6 @@
     back_x,
     ready,
     loaded,
-    stored,
     data_sent,
     data_here,
     ids_sent,
@@ -248,7 +245,7 @@
 
         def edge(v, tile, bx):
             return jnp.concatenate(
-                [measured[v, tile, pl.ds(q * 8 + bx, 8, stride=32), :] for q in range(4)], axis=0
+                [measured[plane, v, tile, pl.ds(q * 8 + bx, 8, stride=32), :] for q in range(4)], axis=0
             )
 
         for at, bx, corner in ((0, 7, 512), (128, 0, 576)):
@@ -280,7 +277,7 @@
         for v in range(2):
             for x8 in range(8):
                 at, back = 64 * v + 32 * (x8 // 4), -32 * (x8 % 4)
-                measured[v, 2, pl.ds(32 * x8, 32), :] = sides(
+                measured[plane, v, 2, pl.ds(32 * x8, 32), :] = sides(
                     turn(got(256 + at), back), turn(got(384 + at), back + 32)
                 )
             for row, start, corner, there in (
@@ -288,10 +285,10 @@
                 (TILE + 32, 128, 576, has_high_x),
             ):
                 for tile in range(2):
-                    measured[v, tile, pl.ds(row, 32), :] = (
+                    measured[plane, v, tile, pl.ds(row, 32), :] = (
                         got(start + 64 * v + 32 * tile) * there
                     )
-                measured[v, 2, pl.ds(row, 32), :] = (
+                measured[plane, v, 2, pl.ds(row, 32), :] = (
                     sides(
                         turn(got(corner), 32 + 32 * v), turn(got(corner + 32), 32 - 32 * v)
                     )
@@ -347,20 +344,22 @@
     for plane in range(2):
         pack_estimate(plane)
 
+    def pick_group(plane, group):
+        rows = GROUP * 16
+        wanted = iota((rows, 1024), 0) + group * rows
+        pick = jnp.where(wanted == target, 1.0, 0.0).astype(BF16)
+        outgoing[plane, pl.ds(pl.multiple_of(group * rows, rows), rows), :] = dot(
+            pick, staged[plane]
+        ).astype(BF16)
+
+    @pl.loop(0, GROUPS)
+    def _(group):
+        pick_group(0, group)
+
     pl.semaphore_wait(barrier, N_GX + N_GY - 2)
     for step in range(1, N_GY):
         pl.semaphore_signal(
             ready, inc=1, device_id=(gx, (gy + step) % N_GY), device_id_type=MESH
-        )
-    pl.semaphore_wait(ready, N_GY - 1)
-
-    for plane in range(2):
-        send_parts(
-            ESTIMATE_PARTS,
-            estimate_out.at[plane],
-            estimate_halo.at[plane],
-            estimate_sent.at[plane],
-            estimate_here.at[plane],
         )
 
     def id_copy(slot):
@@ -384,41 +383,53 @@
             device_id_type=MESH,
         )
 
+    def send_group(group):
+        for j in range(GROUP):
+            if j == 0:
+
+                @pl.when(group > 0)
+                def _():
+                    data_copy(1, group * GROUP).start()
+
+            else:
+                data_copy(1, group * GROUP + j).start()
+
+    def send_first(to_x, to_y):
+        slot = slot_of(to_x * N_GY + to_y, here)
+        id_copy(slot).start()
+        data_copy(0, slot).start()
+
+    @pl.loop(1, N_GY)
+    def _(step):
+        send_first(gx, (gy + step) % N_GY)
+
+    @pl.loop(1, N_GX)
+    def _(step):
+        send_first((gx + step) % N_GX, gy)
+
+    pl.semaphore_wait(ready, N_GY - 1)
+    for plane in range(2):
+        send_parts(
+            ESTIMATE_PARTS,
+            estimate_out.at[plane],
+            estimate_halo.at[plane],
+            estimate_sent.at[plane],
+            estimate_here.at[plane],
+        )
+
     @pl.loop(1, DEVICES)
     def _(slot):
-        id_copy(slot).start()
-
-    def pick_group(plane, group):
-        rows = GROUP * 16
-        wanted = iota((rows, 1024), 0) + group * rows
-        pick = jnp.where(wanted == target, 1.0, 0.0).astype(BF16)
-        outgoing[plane, pl.ds(pl.multiple_of(group * rows, rows), rows), :] = dot(
-            pick, staged[plane]
-        ).astype(BF16)
-
-    def send_group(plane, group):
-        for j in range(GROUP):
-            if j == 0:
-
-                @pl.when(group > 0)
-                def _():
-                    data_copy(plane, group * GROUP).start()
-
-            else:
-                data_copy(plane, group * GROUP + j).start()
-
-    @pl.loop(0, GROUPS)
-    def _(group):
-        pick_group(0, group)
-        send_group(0, group)
+        to_x, to_y = partner(slot, here)
+
+        @pl.when((to_x != gx) & (to_y != gy))
+        def _():
+            id_copy(slot).start()
+            data_copy(0, slot).start()
 
     @pl.loop(0, GROUPS)
     def _(group):
         pick_group(1, group)
-
-        @pl.when(group < EARLY)
-        def _():
-            send_group(1, group)
+        send_group(group)
 
     for load in loads[4:]:
         load.wait()
@@ -555,33 +566,25 @@
                             if by != x4:
                                 moved = pltpu.roll(source[by], ((by - x4) % 4) * 32, 1)
                                 tile = jnp.where(group_of == by, moved, tile)
-                        measured[v, wide, pl.ds((h * 4 + x4) * 32, 32), :] = tile
-
-    def wide_measured(v):
-        return jnp.concatenate([measured[v, tile] for tile in range(3)], axis=1)
-
-    def store(plane):
-        return pltpu.make_async_copy(final.at[plane], result.at[plane], stored.at[plane])
+                        measured[plane, v, wide, pl.ds((h * 4 + x4) * 32, 32), :] = tile
+
+    def wide_measured(plane, v):
+        return jnp.concatenate([measured[plane, v, tile] for tile in range(3)], axis=1)
 
     for plane in range(2):
         land(plane)
         send_others(plane)
-        if plane == 0:
-
-            @pl.loop(EARLY, GROUPS)
-            def _(group):
-                send_group(1, group)
-
+
+    for plane in range(2):
         widen_measured(plane)
-        ratios = [wide_measured(v) * inverse[plane, v] for v in range(2)]
+        ratios = [wide_measured(plane, v) * inverse[plane, v] for v in range(2)]
         current = wide_estimate[plane] * (0.5 * correction(ratios, plane, WIDE, LANES))
         ratios = [
-            wide_measured(v) / blurred for v, blurred in enumerate(forward(current, plane))
+            wide_measured(plane, v) / blurred for v, blurred in enumerate(forward(current, plane))
         ]
-        final[plane] = current[:TILE, :TILE] * (
+        result[plane] = current[:TILE, :TILE] * (
             0.5 * correction(ratios, plane, TILE, TILE)
         )
-        store(plane).start()
 
     rest = ids_out.at[pl.ds(1, DEVICES - 1)]
     pltpu.make_async_copy(rest, rest, ids_sent).wait()
@@ -592,18 +595,17 @@
         pltpu.make_async_copy(whole, whole, estimate_sent.at[plane]).wait()
         whole = measured_out.at[plane]
         pltpu.make_async_copy(whole, whole, measured_sent.at[plane]).wait()
-        store(plane).wait()
 
 
 def shards(blocks, owner_route, block_slot, estimate, background, psf_taps, psf_index):
     owners = owner_route.reshape(owner_route.shape[:2])
-    anywhere = pl.BlockSpec(memory_space=pl.ANY)
+    far = pl.BlockSpec(memory_space=pltpu.HBM)
     dma = pltpu.SemaphoreType.DMA
     return pl.pallas_call(
         kernel,
         out_shape=jax.ShapeDtypeStruct(estimate.shape, F32),
-        in_specs=[anywhere] * 7,
-        out_specs=anywhere,
+        in_specs=[far] * 7,
+        out_specs=pl.BlockSpec(memory_space=pltpu.VMEM),
         scratch_shapes=[
             pltpu.VMEM(blocks.shape, BF16),
             pltpu.VMEM(owners.shape, jnp.int32),
@@ -620,9 +622,8 @@
             pltpu.VMEM((512, DEVICES * 16), BF16),
             pltpu.VMEM((512, 256), F32),
             pltpu.VMEM((2, WIDE, LANES), F32),
-            pltpu.VMEM((2, 3, WIDE, 128), F32),
+            pltpu.VMEM((2, 2, 3, WIDE, 128), F32),
             pltpu.VMEM((2, 2, WIDE, LANES), F32),
-            pltpu.VMEM((2, TILE, TILE), F32),
             pltpu.VMEM((4, WIDE, 128), F32),
             pltpu.VMEM((2, ESTIMATE_ROWS, 128), BF16),
             pltpu.VMEM((2, ESTIMATE_ROWS, 128), BF16),
@@ -635,7 +636,6 @@
             pltpu.SemaphoreType.REGULAR,
             dma((7,)),
             dma((2,)),
-            dma((2,)),
             dma((2, GROUPS)),
             dma,
             dma,
@@ -645,7 +645,7 @@
             dma((2,)),
         ],
         compiler_params=pltpu.CompilerParams(
-            collective_id=0, has_side_effects=True, vmem_limit_bytes=48 << 20
+            collective_id=0, has_side_effects=True, vmem_limit_bytes=62 << 20
         ),
         cost_estimate=pl.CostEstimate(
             flops=8_000_000_000, bytes_accessed=2 << 20, transcendentals=0

time: 72 us -> 53.2 us (0.74)
  Pallas kernels: 65.3 us -> 51.1 us
  local copies, waits for them, and re-layouts: 6.47 us -> 1.87 us
    pallas_call x1, Pallas kernels: 65.3 us -> 51.1 us  [shards(): pl.pallas_call(kernel, out_shape=jax.ShapeDtypeStruct(estimate.shape, F32...]
    unnamed x15 -> x1, local copies, waits for them, and re-layouts: 6.47 us -> 1.87 us
where the time goes in v2:
time: 53.2 us; the launch traced here: 53 us
  Pallas kernels  51.1 us (96%)
  local copies, waits for them, and re-layouts  1.87 us (4%)
    pallas_call x1, Pallas kernels, shards(): pl.pallas_call(kernel, out_shape=jax.ShapeDtypeStruct(estimate.shape, F32...  51.1 us
    unnamed x1, local copies, waits for them, and re-layouts  1.87 us

profile of v2, /device:TPU:0, one launch (start us, length us, event | category | flops | bytes accessed | tf_op | source)
XLA Modules:
  0.0 53.0 jit_solution(7865419860960403341)
XLA Ops:
  0.0 51.1 %shard_map.73 = f32[2,256,256]{2,1,0:T(8,128)} custom-call(bf16[2,128,2048]{2,1,0:T(8,128)(2,1)} %blocks_in.1, s32[2,128]{1,0:T(2,128)} %bitcast.1, s32[2,128]{1,0:T(2,128)} %places_in.1, f32[2,256,256]{2,1,0:T(8,128)} %estimate_in.1, f32[2,2]{1,0:T(2,128)} %background_in.1, f32[2,4,2,17]{3,2,1,0:T(2,128)} %taps_in.1, s32[2,2]{1,0:T(2,128)} %index_in.1), custom_call_target="tpu_custom_call" | custom-call | flops 8000000000 | bytes 2097152 | tf_op jit(solution)/shard_map/pallas_call | solution.py:604
  51.1 1.9 %copy.9 = f32[2,256,256]{2,1,0:T(8,128)} copy(f32[2,256,256]{2,1,0:T(8,128)} %shard_map.73) | data formatting | bytes 1048576

commit v3 on v2

--- a/solution.py
+++ b/solution.py
@@ -23,12 +23,12 @@
     (64, 64, -1, 0),
     (128, 64, 0, 1),
     (192, 64, 0, -1),
-    (256, 32, 1, 1),
-    (288, 32, 1, -1),
-    (320, 32, -1, 1),
-    (352, 32, -1, -1),
+    (256, 16, 1, 1),
+    (272, 16, 1, -1),
+    (288, 16, -1, 1),
+    (304, 16, -1, -1),
 )
-ESTIMATE_ROWS = 384
+ESTIMATE_ROWS = 320
 SIDE_PARTS = ((256, 128, 0, 1), (384, 128, 0, -1))
 OTHER_PARTS = (
     (0, 128, 1, 0),
@@ -146,11 +146,11 @@
     for load in loads:
         load.start()
 
-    for step in range(1, N_GX):
+    for step in (6, 10, 7, 9, 8, 2, 14, 3, 13, 5, 11, 4, 12, 15, 1):
         pl.semaphore_signal(
             barrier, inc=1, device_id=((gx + step) % N_GX, gy), device_id_type=MESH
         )
-    for step in range(1, N_GY):
+    for step in (5, 3, 4, 6, 2, 7, 1):
         pl.semaphore_signal(
             barrier, inc=1, device_id=(gx, (gy + step) % N_GY), device_id_type=MESH
         )
@@ -166,9 +166,10 @@
 
     def sides(low, high):
         at = iota(low.shape, 1)
-        return jnp.where(
+        both = jnp.where(
             at < 32, low * has_low_y, jnp.where(at < 64, high * has_high_y, 0.0)
         )
+        return both + turn(both, 64)
 
     def send_parts(parts, out, into, sent, arrived):
         for start, rows, to_x, to_y in parts:
@@ -195,10 +196,14 @@
                 moved = turn(piece, 32 * slab + 32 * tile)
                 packed = jnp.where(iota((64, 128), 1) // 32 == slab, moved, packed)
             out[pl.ds(at, 64)] = packed.astype(BF16)
-        for at, row, tile in ((256, 224, 1), (288, 224, 0), (320, 0, 1), (352, 0, 0)):
-            out[pl.ds(at, 32)] = estimate[
-                plane, pl.ds(row, 32), pl.ds(128 * tile, 128)
-            ].astype(BF16)
+        for at, row, tile in ((256, 224, 1), (272, 224, 0), (288, 0, 1), (304, 0, 0)):
+            top, bottom = (
+                estimate[plane, pl.ds(row + 16 * half, 16), pl.ds(128 * tile, 128)]
+                for half in range(2)
+            )
+            at_lane = iota((16, 128), 1)
+            top, bottom = turn(top, 32 * tile), turn(bottom, 32 + 32 * tile)
+            out[pl.ds(at, 16)] = jnp.where(at_lane < 32, top, bottom).astype(BF16)
 
     def widen_estimate(plane):
         whole = estimate_halo.at[plane]
@@ -215,15 +220,15 @@
             )
         for row, start, corner, there in (
             (TILE, 0, 256, has_low_x),
-            (TILE + 32, 64, 320, has_high_x),
+            (TILE + 32, 64, 288, has_high_x),
         ):
             for tile in range(2):
                 wide[pl.ds(row, 32), pl.ds(128 * tile, 128)] = (
                     got(start + 32 * tile, 32) * there
                 )
-            wide[pl.ds(row, 32), pl.ds(TILE, 128)] = (
-                sides(turn(got(corner, 32), 32), turn(got(corner + 32, 32), 32)) * there
-            )
+            low, high = got(corner, 16), got(corner + 16, 16)
+            wide[pl.ds(row, 16), pl.ds(TILE, 128)] = sides(low, turn(high, 32)) * there
+            wide[pl.ds(row + 16, 16), pl.ds(TILE, 128)] = sides(turn(low, -32), high) * there
 
     def send_sides(plane):
         for at, by in ((256, 7), (384, 0)):
@@ -407,15 +412,19 @@
     def _(step):
         send_first((gx + step) % N_GX, gy)
 
+    def send_estimate(parts):
+        for plane in range(2):
+            send_parts(
+                parts,
+                estimate_out.at[plane],
+                estimate_halo.at[plane],
+                estimate_sent.at[plane],
+                estimate_here.at[plane],
+            )
+
+    send_estimate(ESTIMATE_PARTS[:4])
     pl.semaphore_wait(ready, N_GY - 1)
-    for plane in range(2):
-        send_parts(
-            ESTIMATE_PARTS,
-            estimate_out.at[plane],
-            estimate_halo.at[plane],
-            estimate_sent.at[plane],
-            estimate_here.at[plane],
-        )
+    send_estimate(ESTIMATE_PARTS[4:])
 
     @pl.loop(1, DEVICES)
     def _(slot):
@@ -452,7 +461,7 @@
         side = jnp.where(
             at < 32, turn(m[:, :128], 32), jnp.where(at < 64, turn(m[:, 384:], 32), 0.0)
         )
-        return jnp.concatenate([m[:, 128:384], side], axis=1)
+        return jnp.concatenate([m[:, 128:384], side + turn(side, 64)], axis=1)
 
     def by_rows(m):
         return jnp.concatenate([m[32 : 32 + TILE], m[:32], m[32 + TILE :]], axis=0)
@@ -473,47 +482,54 @@
         ]
         return jnp.concatenate(main + [m[:32], m[32 + TILE :]], axis=0)
 
-    def put(ref, index, value):
-        high, low = split(value)
-        ref[(0,) + index] = high
-        ref[(1,) + index] = low
-
+    def rounded_sum(first):
+        return jnp.sum(first[0:1].astype(BF16).astype(F32), axis=1, keepdims=True)
+
+    scales = []
     for plane in range(2):
         for v in range(2):
             m = by_lanes(by_rows(bands(v, plane, 1, True)))
-            put(fwd_y, (plane, slice(None), pl.ds(v * LANES, LANES)), m)
-            put(back_y, (plane, v), by_lanes(by_rows(bands(v, plane, 1, False))))
-            m = by_lanes(reordered(bands(v, plane, 0, False)))
-            put(fwd_x, (plane, v), m[:, :WIDE])
+            fwd_y[plane, :, pl.ds(v * LANES, LANES)] = m.astype(BF16)
+            m = bands(v, plane, 1, False)
+            scale = rounded_sum(m)
+            high, low = split(by_lanes(by_rows(m)))
+            back_y[plane, v] = jnp.concatenate([high, low[TILE:], low[:TILE]], axis=0)
+            m = bands(v, plane, 0, False)
+            scales.append(1.0 / (scale * rounded_sum(m)))
+            m = by_lanes(reordered(m))
+            fwd_x[plane, v] = m[:, :WIDE].astype(BF16)
             square = jnp.concatenate([m, jnp.zeros((LANES - WIDE, LANES), F32)], axis=0)
-            put(back_x, (plane, v), square.T[:WIDE, :WIDE])
+            high, low = split(square.T[:WIDE])
+            side = high[:, TILE:].astype(F32)
+            side = (side + turn(side, 64)).astype(BF16)
+            for at, piece in (
+                (0, high[:, :TILE]),
+                (TILE, high[:, :TILE]),
+                (2 * TILE, low[:, :TILE]),
+                (3 * TILE, side),
+                (3 * TILE + 128, low[:, TILE:]),
+            ):
+                back_x[plane, v, :, pl.ds(at, piece.shape[1])] = piece
 
     def forward(field, plane):
         field = field.astype(BF16)[:, :WIDE]
-        along_y = (dot(field, fwd_y[0, plane]) + dot(field, fwd_y[1, plane])).astype(BF16)
-        blurred = []
-        for v in range(2):
-            mine = along_y[:, v * LANES : (v + 1) * LANES]
-            blurred.append(
-                dot(fwd_x[0, plane, v], mine)
-                + dot(fwd_x[1, plane, v], mine)
-                + background[v, plane]
-            )
-        return blurred
+        along_y = dot(field, fwd_y[plane]).astype(BF16)
+        return [
+            dot(fwd_x[plane, v], along_y[:, v * LANES : (v + 1) * LANES])
+            * scales[2 * plane + v]
+            + background[v, plane]
+            for v in range(2)
+        ]
 
     def correction(ratios, plane, rows, lanes):
         total = jnp.zeros((rows, lanes), F32)
         for v in range(2):
-            ratio = ratios[v].astype(BF16)[:, :WIDE]
-            high, low = split(
-                dot(ratio, back_y[0, plane, v][:, :lanes])
-                + dot(ratio, back_y[1, plane, v][:, :lanes])
-            )
-            total = (
-                total
-                + dot(back_x[0, plane, v][:rows], high)
-                + dot(back_x[0, plane, v][:rows], low)
-                + dot(back_x[1, plane, v][:rows], high)
+            ratio = ratios[v].astype(BF16)
+            ratio = jnp.concatenate([ratio, ratio[:, :TILE]], axis=1)
+            high, low = split(dot(ratio, back_y[plane, v][:, :lanes]))
+            stack = [high[:TILE], low[:TILE], high[:TILE], high[TILE:], low[TILE:], high[TILE:]]
+            total = total + dot(
+                back_x[plane, v][:rows, : 3 * WIDE], jnp.concatenate(stack, axis=0)
             )
         return total
 
@@ -629,10 +645,10 @@
             pltpu.VMEM((2, ESTIMATE_ROWS, 128), BF16),
             pltpu.VMEM((2, MEASURED_ROWS, 128), BF16),
             pltpu.VMEM((2, MEASURED_ROWS, 128), BF16),
-            pltpu.VMEM((2, 2, WIDE, 2 * LANES), BF16),
-            pltpu.VMEM((2, 2, 2, WIDE, WIDE), BF16),
-            pltpu.VMEM((2, 2, 2, WIDE, LANES), BF16),
-            pltpu.VMEM((2, 2, 2, WIDE, WIDE), BF16),
+            pltpu.VMEM((2, WIDE, 2 * LANES), BF16),
+            pltpu.VMEM((2, 2, WIDE, WIDE), BF16),
+            pltpu.VMEM((2, 2, 2 * WIDE, LANES), BF16),
+            pltpu.VMEM((2, 2, WIDE, 1024), BF16),
             pltpu.SemaphoreType.REGULAR,
             dma((7,)),
             dma((2,)),

time: 53.2 us -> 50.7 us (0.953)
  Pallas kernels: 51.1 us -> 48.3 us
    pallas_call x1, Pallas kernels: 51.1 us -> 48.3 us  [shards(): pl.pallas_call(kernel, out_shape=jax.ShapeDtypeStruct(estimate.shape, F32...]
where the time goes in v3:
time: 50.7 us; the launch traced here: 50.2 us
  Pallas kernels  48.3 us (95%)
  local copies, waits for them, and re-layouts  1.87 us (4%)
    pallas_call x1, Pallas kernels, shards(): pl.pallas_call(kernel, out_shape=jax.ShapeDtypeStruct(estimate.shape, F32...  48.3 us
    unnamed x1, local copies, waits for them, and re-layouts  1.87 us

profile of v3, /device:TPU:0, one launch (start us, length us, event | category | flops | bytes accessed | tf_op | source)
XLA Modules:
  0.0 50.2 jit_solution(16478432253760029725)
XLA Ops:
  0.0 48.3 %shard_map.73 = f32[2,256,256]{2,1,0:T(8,128)} custom-call(bf16[2,128,2048]{2,1,0:T(8,128)(2,1)} %blocks_in.1, s32[2,128]{1,0:T(2,128)} %bitcast.1, s32[2,128]{1,0:T(2,128)} %places_in.1, f32[2,256,256]{2,1,0:T(8,128)} %estimate_in.1, f32[2,2]{1,0:T(2,128)} %background_in.1, f32[2,4,2,17]{3,2,1,0:T(2,128)} %taps_in.1, s32[2,2]{1,0:T(2,128)} %index_in.1), custom_call_target="tpu_custom_call" | custom-call | flops 8000000000 | bytes 2097152 | tf_op jit(solution)/shard_map/pallas_call | solution.py:620
  48.3 1.9 %copy.9 = f32[2,256,256]{2,1,0:T(8,128)} copy(f32[2,256,256]{2,1,0:T(8,128)} %shard_map.73) | data formatting | bytes 1048576

commit v4 on v3

--- a/solution.py
+++ b/solution.py
@@ -29,16 +29,16 @@
     (304, 16, -1, -1),
 )
 ESTIMATE_ROWS = 320
-SIDE_PARTS = ((256, 128, 0, 1), (384, 128, 0, -1))
+SIDE_PARTS = ((192, 128, 0, 1), (320, 128, 0, -1))
 OTHER_PARTS = (
-    (0, 128, 1, 0),
-    (128, 128, -1, 0),
-    (512, 32, 1, 1),
-    (544, 32, 1, -1),
-    (576, 32, -1, 1),
-    (608, 32, -1, -1),
+    (0, 96, 1, 0),
+    (96, 96, -1, 0),
+    (448, 16, 1, 1),
+    (464, 16, 1, -1),
+    (480, 16, -1, 1),
+    (496, 16, -1, -1),
 )
-MEASURED_ROWS = 640
+MEASURED_ROWS = 512
 
 
 def iota(shape, dim):
@@ -105,6 +105,7 @@
     wide_estimate,
     measured,
     inverse,
+    final,
     shuffle,
     estimate_out,
     estimate_halo,
@@ -116,6 +117,7 @@
     back_x,
     ready,
     loaded,
+    stored,
     data_sent,
     data_here,
     ids_sent,
@@ -143,9 +145,6 @@
             )
         )
     ]
-    for load in loads:
-        load.start()
-
     for step in (6, 10, 7, 9, 8, 2, 14, 3, 13, 5, 11, 4, 12, 15, 1):
         pl.semaphore_signal(
             barrier, inc=1, device_id=((gx + step) % N_GX, gy), device_id_type=MESH
@@ -154,6 +153,9 @@
         pl.semaphore_signal(
             barrier, inc=1, device_id=(gx, (gy + step) % N_GY), device_id_type=MESH
         )
+
+    for load in loads:
+        load.start()
 
     has_low_x = jnp.where(gx > 0, 1.0, 0.0)
     has_high_x = jnp.where(gx < N_GX - 1, 1.0, 0.0)
@@ -231,7 +233,7 @@
             wide[pl.ds(row + 16, 16), pl.ds(TILE, 128)] = sides(turn(low, -32), high) * there
 
     def send_sides(plane):
-        for at, by in ((256, 7), (384, 0)):
+        for at, by in ((192, 7), (320, 0)):
             for v in range(2):
                 for h in range(2):
                     measured_out[plane, pl.ds(at + 64 * v + 32 * h, 32)] = summed[
@@ -253,17 +255,21 @@
                 [measured[plane, v, tile, pl.ds(q * 8 + bx, 8, stride=32), :] for q in range(4)], axis=0
             )
 
-        for at, bx, corner in ((0, 7, 512), (128, 0, 576)):
-            for tile in range(2):
-                edges = [edge(v, tile, bx) for v in range(2)]
-                for v in range(2):
-                    out[pl.ds(at + 64 * v + 32 * tile, 32)] = edges[v].astype(BF16)
-                if tile == 1:
-                    both = jnp.where(narrow >= 96, edges[0], turn(edges[1], 96))
-                    out[pl.ds(corner, 32)] = both.astype(BF16)
-                else:
-                    both = jnp.where(narrow < 32, edges[0], turn(edges[1], 32))
-                    out[pl.ds(corner + 32, 32)] = both.astype(BF16)
+        for at, bx, corner, first in ((0, 7, 448, 8), (96, 0, 480, 0)):
+            edges = [[edge(v, tile, bx) for tile in range(2)] for v in range(2)]
+            out[pl.ds(at, 96)] = jnp.concatenate(
+                [edges[v][tile][first : first + 24] for v in range(2) for tile in range(2)],
+                axis=0,
+            ).astype(BF16)
+            for start, tile in ((corner, 1), (corner + 16, 0)):
+                both = jnp.where(
+                    narrow < 32,
+                    turn(edges[0][tile], 32 * tile),
+                    turn(edges[1][tile], 32 + 32 * tile),
+                )
+                out[pl.ds(start, 16)] = jnp.where(
+                    narrow[:16] < 64, both[:16], turn(both[16:], 64)
+                ).astype(BF16)
         send_parts(
             OTHER_PARTS,
             measured_out.at[plane],
@@ -276,29 +282,30 @@
         whole = measured_halo.at[plane]
         pltpu.make_async_copy(whole, whole, measured_here.at[plane]).wait()
 
-        def got(start):
-            return measured_halo[plane, pl.ds(start, 32)].astype(F32)
+        def got(start, rows):
+            return measured_halo[plane, pl.ds(start, rows)].astype(F32)
 
         for v in range(2):
             for x8 in range(8):
                 at, back = 64 * v + 32 * (x8 // 4), -32 * (x8 % 4)
                 measured[plane, v, 2, pl.ds(32 * x8, 32), :] = sides(
-                    turn(got(256 + at), back), turn(got(384 + at), back + 32)
+                    turn(got(192 + at, 32), back), turn(got(320 + at, 32), back + 32)
                 )
-            for row, start, corner, there in (
-                (TILE, 0, 512, has_low_x),
-                (TILE + 32, 128, 576, has_high_x),
-            ):
+        for row, first, start, corner, there in (
+            (TILE, TILE + 8, 0, 448, has_low_x),
+            (TILE + 32, TILE + 32, 96, 480, has_high_x),
+        ):
+            rows = got(start, 96) * there
+            low, high = got(corner, 16), got(corner + 16, 16)
+            for v in range(2):
                 for tile in range(2):
-                    measured[plane, v, tile, pl.ds(row, 32), :] = (
-                        got(start + 64 * v + 32 * tile) * there
+                    at = 48 * v + 24 * tile
+                    measured[plane, v, tile, pl.ds(first, 24), :] = rows[at : at + 24]
+                for half in range(2):
+                    back = -32 * v - 64 * half
+                    measured[plane, v, 2, pl.ds(row + 16 * half, 16), :] = (
+                        sides(turn(low, back), turn(high, back + 32)) * there
                     )
-                measured[plane, v, 2, pl.ds(row, 32), :] = (
-                    sides(
-                        turn(got(corner), 32 + 32 * v), turn(got(corner + 32), 32 - 32 * v)
-                    )
-                    * there
-                )
 
     loads[0].wait()
     loads[1].wait()
@@ -538,6 +545,12 @@
         for v, blurred in enumerate(forward(wide_estimate[plane], plane)):
             inverse[plane, v] = 1.0 / blurred
 
+    for plane in range(2):
+        for v in range(2):
+            for tile in range(2):
+                measured[plane, v, tile, pl.ds(TILE, 8), :] = jnp.zeros((8, 128), F32)
+                measured[plane, v, tile, pl.ds(WIDE - 8, 8), :] = jnp.zeros((8, 128), F32)
+
     rest = ids_in.at[pl.ds(1, DEVICES - 1)]
     pltpu.make_async_copy(rest, rest, ids_here).wait()
     ids_in[pl.ds(0, 1)] = ids_out[pl.ds(0, 1)]
@@ -587,6 +600,9 @@
     def wide_measured(plane, v):
         return jnp.concatenate([measured[plane, v, tile] for tile in range(3)], axis=1)
 
+    def store(plane):
+        return pltpu.make_async_copy(final.at[plane], result.at[plane], stored.at[plane])
+
     for plane in range(2):
         land(plane)
         send_others(plane)
@@ -598,9 +614,10 @@
         ratios = [
             wide_measured(plane, v) / blurred for v, blurred in enumerate(forward(current, plane))
         ]
-        result[plane] = current[:TILE, :TILE] * (
+        final[plane] = current[:TILE, :TILE] * (
             0.5 * correction(ratios, plane, TILE, TILE)
         )
+        store(plane).start()
 
     rest = ids_out.at[pl.ds(1, DEVICES - 1)]
     pltpu.make_async_copy(rest, rest, ids_sent).wait()
@@ -611,6 +628,7 @@
         pltpu.make_async_copy(whole, whole, estimate_sent.at[plane]).wait()
         whole = measured_out.at[plane]
         pltpu.make_async_copy(whole, whole, measured_sent.at[plane]).wait()
+        store(plane).wait()
 
 
 def shards(blocks, owner_route, block_slot, estimate, background, psf_taps, psf_index):
@@ -621,7 +639,7 @@
         kernel,
         out_shape=jax.ShapeDtypeStruct(estimate.shape, F32),
         in_specs=[far] * 7,
-        out_specs=pl.BlockSpec(memory_space=pltpu.VMEM),
+        out_specs=far,
         scratch_shapes=[
             pltpu.VMEM(blocks.shape, BF16),
             pltpu.VMEM(owners.shape, jnp.int32),
@@ -640,6 +658,7 @@
             pltpu.VMEM((2, WIDE, LANES), F32),
             pltpu.VMEM((2, 2, 3, WIDE, 128), F32),
             pltpu.VMEM((2, 2, WIDE, LANES), F32),
+            pltpu.VMEM((2, TILE, TILE), F32),
             pltpu.VMEM((4, WIDE, 128), F32),
             pltpu.VMEM((2, ESTIMATE_ROWS, 128), BF16),
             pltpu.VMEM((2, ESTIMATE_ROWS, 128), BF16),
@@ -651,6 +670,7 @@
             pltpu.VMEM((2, 2, WIDE, 1024), BF16),
             pltpu.SemaphoreType.REGULAR,
             dma((7,)),
+            dma((2,)),
             dma((2,)),
             dma((2, GROUPS)),
             dma,

time: 50.7 us -> 50.4 us (level)
  no operation moved by 1% of the time
where the time goes in v4:
time: 50.4 us; the launch traced here: 50.1 us
  Pallas kernels  48.3 us (96%)
  local copies, waits for them, and re-layouts  1.87 us (4%)
    pallas_call x1, Pallas kernels, shards(): pl.pallas_call(kernel, out_shape=jax.ShapeDtypeStruct(estimate.shape, F32...  48.3 us
    unnamed x1, local copies, waits for them, and re-layouts  1.87 us

profile of v4, /device:TPU:0, one launch (start us, length us, event | category | flops | bytes accessed | tf_op | source)
XLA Modules:
  0.0 50.1 jit_solution(8640667873258400261)
XLA Ops:
  0.0 48.3 %shard_map.73 = f32[2,256,256]{2,1,0:T(8,128)} custom-call(bf16[2,128,2048]{2,1,0:T(8,128)(2,1)} %blocks_in.1, s32[2,128]{1,0:T(2,128)} %bitcast.1, s32[2,128]{1,0:T(2,128)} %places_in.1, f32[2,256,256]{2,1,0:T(8,128)} %estimate_in.1, f32[2,2]{1,0:T(2,128)} %background_in.1, f32[2,4,2,17]{3,2,1,0:T(2,128)} %taps_in.1, s32[2,2]{1,0:T(2,128)} %index_in.1), custom_call_target="tpu_custom_call" | custom-call | flops 8000000000 | bytes 2097152 | tf_op jit(solution)/shard_map/pallas_call | solution.py:638
  48.3 1.9 %copy.9 = f32[2,256,256]{2,1,0:T(8,128)} copy(f32[2,256,256]{2,1,0:T(8,128)} %shard_map.73) | data formatting | bytes 1048576
